TPU v7x, 128 devices: a whole 4x4x4 slice. The times are simulated.
128 devices in a mesh: box: 8 (over z, core), dir: 16 (over x, y).
Axes of the slice: x: 4, y: 4, z: 4, core: 2. Of those that a mesh axis runs over, the one named last changes fastest.
Arguments:
- currents: bfloat16 [16384, 256, 128], P(('box', 'dir')), may hold values from -6 to 6
- leaf_parent: int32 [16384], P(('box', 'dir')), may hold values from 0 to 255, as said below
- near_links: int32 [16384, 2], P(('box', 'dir')), may hold values 0 or 1
- near_blocks: bfloat16 [3, 256, 256], replicated, may hold values from -0.375 to 0.375
- aggregate_maps: bfloat16 [64, 256, 256], replicated, may hold values from -0.375 to 0.375
- far_boxes: int32 [256, 64], P('box'), may hold values from 0 to 255
- far_counts: int32 [256], P('box'), may hold values from 16 to 64
- translate_coef: float32 [256, 64, 256], P('box'), may hold values from 0.005 to 0.05
- time_kernel: float32 [128], replicated, may hold values from -0.5 to 0.5
- disaggregate_maps: bfloat16 [64, 256, 256], replicated, may hold values from -0.375 to 0.375
Outputs:
- field: bfloat16 [16384, 256, 128], P(('box', 'dir'))
Inputs may be any that keep to these rules, and one draw needn't show every extreme that they name: `leaf_parent`: the leaves k * 64 to (k + 1) * 64 - 1 share one parent. The leaves g * 2048 to (g + 1) * 2048 - 1 have as parents the top-level boxes g * 32 to (g + 1) * 32 - 1, each exactly once as a run.
All inputs are finite; a program needn't handle non-finite values. No bound on the sum of `near_links` on one device may be relied on, other than what follows from the above.
Results may differ from a plain program's by a relative error of at most 0.0047.
Values may be sent and summed in bfloat16 or wider, within the bound.
No kernel may reach another device: no remote copies, remote signals or barrier semaphores. Data moves between devices by JAX's collectives and lax.ppermute only.
A program may use at most 192 MiB of HBM per device.

v0:
```python
import jax
import jax.numpy as jnp
from jax import lax
from jax.sharding import Mesh
from jax.sharding import PartitionSpec as P

LEAF_TOP = 64
BOX = ("box_0", "box_1")
BOX_DIR = ("box_0", "box_1", "dir")


def in_blocks(array, dim, devices):
    before, after = (array.shape[:dim], array.shape[dim + 1 :])
    return jnp.moveaxis(array.reshape(*before, devices, -1, *after), dim, 0)


def summed_on_arrival(array, axis, dim):
    tiles = in_blocks(array, dim, lax.axis_size(axis))
    arrived = lax.all_to_all(tiles, axis, split_axis=0, concat_axis=0, tiled=True)
    return arrived.sum(axis=0)


def edges_of(length, count):
    unit = 8 if length >= 8 * count else 1
    return [length // unit * k // count * unit for k in range(1, count)]


def all_blocks(array, axes, sequence):
    tiles = array[None]
    for k in sequence:
        tiles = lax.all_gather(tiles, axes[k], axis=0, tiled=True)
    held = [lax.axis_size(axes[k]) for k in reversed(sequence)]
    tiles = tiles.reshape(*held, *array.shape)
    turned = sorted(range(len(sequence)), key=lambda place: sequence[len(sequence) - 1 - place])
    return tiles.transpose(*turned, *range(len(sequence), tiles.ndim)).reshape(-1, *array.shape)


def in_order(tiles, dim):
    shape = list(tiles.shape[1:])
    shape[dim] *= tiles.shape[0]
    return jnp.moveaxis(tiles, 0, dim).reshape(shape)


def spread_gather(array, axes, dim):
    numbers = list(range(len(axes)))[::-1]
    cut = array.shape.index(max(array.shape[:-1] or array.shape))
    edges = [0, *edges_of(array.shape[cut], len(axes)), array.shape[cut]]
    done = []
    for k, (start, end) in enumerate(zip(edges, edges[1:])):
        if end > start:
            share = lax.slice_in_dim(array, start, end, axis=cut)
            done.append(all_blocks(share, axes, numbers[k:] + numbers[:k]))
    return in_order(jnp.concatenate(done, axis=cut + 1), dim)


def sent_to_all(array, axis):
    devices = lax.axis_size(axis)
    return lax.all_to_all(
        jnp.broadcast_to(array[None], (devices, *array.shape)), axis, 0, 0, tiled=True
    )


def collect(array, axis, dim):
    return in_order(sent_to_all(array, axis), dim)


def with_halo(block, sides, width):
    for axis, dim in sides:
        count = lax.axis_size(axis)
        forward = [(i, i + 1) for i in range(count - 1)]
        backward = [(target, source) for source, target in forward]
        low = lax.ppermute(
            lax.slice_in_dim(block, block.shape[dim] - width, None, axis=dim), axis, forward
        )
        high = lax.ppermute(lax.slice_in_dim(block, 0, width, axis=dim), axis, backward)
        block = jnp.concatenate([low, block, high], axis=dim)
    return block


def time_matrix(kernel):
    length = kernel.shape[0]
    sample_lag = jnp.arange(length)[:, None] - jnp.arange(length)[None, :]
    return jnp.where(
        sample_lag >= 0, kernel[jnp.clip(sample_lag, 0, length - 1)], jnp.zeros((), kernel.dtype)
    )


def per_device(
    currents,
    leaf_parent,
    near_links,
    near_blocks,
    aggregate_maps,
    far_boxes,
    far_counts,
    translate_coef,
    time_kernel,
    disaggregate_maps,
):
    highest = lax.Precision.HIGHEST
    leaf_count, unknowns, samples = currents.shape
    run_length = min(leaf_count, LEAF_TOP)
    run_count = leaf_count // run_length
    top_local, list_slots = far_boxes.shape
    top_total = top_local * lax.axis_size(BOX)
    direction_total = aggregate_maps.shape[1]
    dir_rows = direction_total // lax.axis_size("dir")
    dir_index = lax.axis_index("dir")
    local_parent = leaf_parent - lax.axis_index(BOX) * top_local
    run_parent = local_parent.reshape(run_count, run_length)[:, 0]
    run_onehot = (run_parent[:, None] == jnp.arange(top_local)[None, :]).astype(jnp.float32)
    leaf_runs = currents.reshape(run_count, run_length, unknowns, samples)
    map_block = aggregate_maps
    run_sums = jnp.einsum("sqp,bspt->bqt", map_block, leaf_runs, preferred_element_type=jnp.float32)
    own_rays = summed_on_arrival(
        jnp.einsum("bc,bqt->qct", run_onehot, run_sums, precision=highest), "dir", 0
    )
    own_rays = own_rays.astype(jnp.bfloat16)
    is_valid = (jnp.arange(list_slots)[None, :] < far_counts[:, None]).astype(jnp.float32)
    matches = (far_boxes[:, :, None] == jnp.arange(top_total)[None, None, :]).astype(
        jnp.float32
    ) * is_valid[:, :, None]
    coef_block = lax.dynamic_slice_in_dim(translate_coef, dir_index * dir_rows, dir_rows, 2)
    weights = jnp.einsum("cfs,cfq->csq", matches, coef_block, precision=highest)
    far_sum = jnp.einsum(
        "csq,qst->cqt",
        weights,
        spread_gather(own_rays, BOX, 1).astype(jnp.float32),
        precision=highest,
    )
    incoming = jnp.einsum(
        "cqs,ts->cqt", far_sum, time_matrix(time_kernel), precision=highest
    ).astype(jnp.bfloat16)
    selected = jnp.einsum(
        "bc,cqt->bqt",
        run_onehot,
        collect(incoming, "dir", 1).astype(jnp.float32),
        precision=highest,
    ).astype(jnp.bfloat16)
    map_block = disaggregate_maps
    far_terms = jnp.einsum("spq,bqt->bspt", map_block, selected, preferred_element_type=jnp.float32)
    far_field = far_terms.reshape(leaf_count, unknowns, samples)
    rim_leaves = jnp.concatenate([currents[:1], currents[-1:]], axis=0)
    extended = with_halo(rim_leaves, ((BOX_DIR, 0),), 1)
    link_mask = near_links.astype(jnp.float32)
    self_term = jnp.einsum(
        "pr,lrt->lpt", near_blocks[0], currents, preferred_element_type=jnp.float32
    )
    before_all = jnp.einsum(
        "pr,lrt->lpt", near_blocks[1], currents, preferred_element_type=jnp.float32
    )
    after_all = jnp.einsum(
        "pr,lrt->lpt", near_blocks[2], currents, preferred_element_type=jnp.float32
    )
    before_rim = jnp.dot(near_blocks[1], extended[0], preferred_element_type=jnp.float32)
    after_rim = jnp.dot(near_blocks[2], extended[3], preferred_element_type=jnp.float32)
    before_term = jnp.concatenate([before_rim[None], before_all[:-1]], axis=0)
    after_term = jnp.concatenate([after_all[1:], after_rim[None]], axis=0)
    near_field = (
        self_term
        + link_mask[:, 0, None, None] * before_term
        + link_mask[:, 1, None, None] * after_term
    )
    return (near_field + far_field).astype(jnp.bfloat16)


def solution(mesh):
    finer = Mesh(mesh.devices.reshape(4, 2, mesh.shape["dir"]), ("box_0", "box_1", "dir"))
    in_specs = (
        P(BOX_DIR, None, None),
        P(BOX_DIR),
        P(BOX_DIR, None),
        P(),
        P(),
        P(BOX, None),
        P(BOX),
        P(BOX, None, None),
        P(),
        P(),
    )
    out_specs = P(BOX_DIR, None, None)
    return jax.shard_map(
        per_device, mesh=finer, in_specs=in_specs, out_specs=out_specs, check_vma=False
    )
```

profile of v0, /device:TPU:34, one launch (start us, length us, event | category | flops | bytes accessed | tf_op | source)
XLA Modules:
  0.0 256.3 jit_solution(14275734861325544151)
XLA Ops:
  0.0 8.3 %fusion.12 = f32[2,256,128]{1,2,0:T(8,128)S(1)} fusion(bf16[2,64,256,128]{3,2,1,0:T(8,128)(2,1)} %bitcast.96, bf16[64,256,256]{2,1,0:T(8,128)(2,1)} %param.14), kind=kOutput, calls=%fused_computation.18 | convolution fusion | flops 2147483648 | bytes 17039360 | tf_op jit(solution)/shard_map/sqp,bspt->bqt/dot_general | solution.py:114
  8.3 0.1 copy.60
  8.5 0.1 reshape.78
  8.6 0.1 slice_reduce_fusion
  8.7 3.9 %fusion.47 = f32[256,128,32]{1,2,0:T(8,128)} fusion(f32[2,256,128]{2,0,1:T(2,128)S(1)} %copy.60, s32[2]{0:T(128)S(1)} %slice_reduce_fusion), kind=kOutput, calls=%fused_computation.56 | convolution fusion | flops 25165888 | bytes 4456456 | tf_op jit(solution)/shard_map/bc,bqt->qct/dot_general | solution.py:116
  12.7 7.5 %all-to-all-start = ((f32[16,16,32,128]{3,2,1,0:T(8,128)}), f32[16,16,32,128]{3,2,1,0:T(8,128)}, u32[]{:S(2)}, u32[]{:S(2)}) async-start(f32[16,16,32,128]{3,2,1,0:T(8,128)} %bitcast.97), calls=%async_computation | async-start | bytes 8388608 | tf_op jit(solution)/shard_map/all_to_all | solution.py:19
  20.1 0.9 fusion.55
  21.0 3.4 %collective-permute-start = (bf16[1,256,128]{2,1,0:T(8,128)(2,1)S(1)}, bf16[1,256,128]{2,1,0:T(8,128)(2,1)S(1)}, u32[]{:S(2)}, u32[]{:S(2)}) collective-permute-start(bf16[1,256,128]{2,1,0:T(8,128)(2,1)S(1)} %get-tuple-element.6), channel_id=1, source_target_pairs={{0,1},{1,2},{2,3},{3,4},{4,5},{5,6},{6,7},{7,8},{8,9},{9,10},{10,1... | collective-permute-start | bytes 196616 | tf_op jit(solution)/shard_map/ppermute | solution.py:72
  24.4 4.6 %collective-permute-start.1 = (bf16[1,256,128]{2,1,0:T(8,128)(2,1)S(1)}, bf16[1,256,128]{2,1,0:T(8,128)(2,1)S(1)}, u32[]{:S(2)}, u32[]{:S(2)}) collective-permute-start(bf16[1,256,128]{2,1,0:T(8,128)(2,1)S(1)} %get-tuple-element.5), channel_id=1, source_target_pairs={{1,0},{2,1},{3,2},{4,3},{5,4},{6,5},{7,6},{8,7},{9,8},{10,9},{11,1... | collective-permute-start | bytes 196616 | tf_op jit(solution)/shard_map/ppermute | solution.py:75
  29.1 97.2 %gather_fusion = f32[16384]{0:T(1024)S(1)} fusion(f32[128]{0:T(128)S(1)} %copy-done.2, s32[16384]{0:T(1024)S(1)} %fusion.39), kind=kCustom, calls=%fused_computation | custom fusion | bytes 196608 | tf_op jit(solution)/shard_map/gather | solution.py:84
  126.4 2.9 %fusion.10 = f32[32,256,16]{1,2,0:T(8,128)S(1)} fusion(f32[32,64,256]{2,1,0:T(8,128)S(1)} %copy-done, s32[]{:T(128)S(6)} %select_n.17, f32[32,64]{1,0:T(8,128)S(1)} %fusion.45, s32[32,64]{1,0:T(8,128)S(1)} %copy-done.6), kind=kOutput, calls=%fused_computation.15 | convolution fusion | flops 101711872 | bytes 1605636 | tf_op jit(solution)/shard_map/cfs,cfq->csq/dot_general | solution.py:124
  129.3 2.6 %reduce_sum.9 = bf16[16,32,128]{2,1,0:T(8,128)(2,1)S(1)} reduce(f32[16,16,32,128]{3,2,1,0:T(8,128)} %all-to-all-done, f32[]{:T(128)} %constant.11.clone.1), dimensions={0}, to_apply=%region_0.0 | reduce | flops 983040 | bytes 4325380 | tf_op jit(solution)/shard_map/reduce_sum | solution.py:20
  132.0 13.3 %all-gather.1 = bf16[64,16,128]{2,1,0:T(8,128)(2,1)S(1)} all-gather(bf16[16,16,128]{2,1,0:T(8,128)(2,1)S(1)} %get-tuple-element.8), channel_id=3, replica_groups=mesh['box_0'=4,'box_1'=2,'dir'=16] {'box_0'}, dimensions={0}, use_global_device_ids=true | all-gather | bytes 327680 | tf_op jit(solution)/shard_map/all_gather | solution.py:31
  145.3 2.2 all_gather.15
  147.5 1.9 all-gather
  149.4 13.4 %all_gather.13 = bf16[8,16,16,128]{3,2,1,0:T(8,128)(2,1)S(1)} all-gather(bf16[2,16,16,128]{3,2,1,0:T(8,128)(2,1)S(1)} %bitcast.103), channel_id=1, replica_groups=mesh['box_0'=4,'box_1'=2,'dir'=16] {'box_0'}, dimensions={0}, use_global_device_ids=true | all-gather | bytes 655360 | tf_op jit(solution)/shard_map/all_gather | solution.py:31
  162.9 0.1 copy.62
  163.0 0.8 convolution_bitcast_fusion.2
  163.8 0.5 convolution_convert_fusion
  164.3 1.7 broadcast_in_dim.36
  166.1 5.5 %all-to-all-start.1 = ((bf16[16,32,16,128]{3,2,1,0:T(8,128)(2,1)}), bf16[16,32,16,128]{3,2,1,0:T(8,128)(2,1)S(1)}, u32[]{:S(2)}, u32[]{:S(2)}) async-start(bf16[16,32,16,128]{3,2,1,0:T(8,128)(2,1)} %broadcast_in_dim.36), calls=%async_computation.1 | async-start | bytes 4194304 | tf_op jit(solution)/shard_map/all_to_all | solution.py:58
  171.6 11.5 %convolution_bitcast_fusion.1 = f32[128,256,128]{1,2,0:T(8,128)} fusion(bf16[128,256,128]{2,1,0:T(8,128)(2,1)} %param.10, bf16[3,256,256]{2,1,0:T(8,128)(2,1)S(1)} %copy-done.3), kind=kOutput, calls=%fused_computation.8 | convolution fusion | flops 2147483648 | bytes 25296896 | tf_op jit(solution)/shard_map/pr,lrt->lpt/dot_general | solution.py:149
  183.1 5.8 %convolution_bitcast_fusion = f32[128,256,128]{1,2,0:T(8,128)S(1)} fusion(bf16[128,256,128]{2,1,0:T(8,128)(2,1)} %param.10, bf16[3,256,256]{2,1,0:T(8,128)(2,1)S(1)} %copy-done.3), kind=kOutput, calls=%fused_computation.7 | convolution fusion | flops 2147483648 | bytes 25296896 | tf_op jit(solution)/shard_map/pr,lrt->lpt/dot_general | solution.py:152
  188.9 11.8 %slice.52 = f32[127,256,128]{1,2,0:T(8,128)} slice(f32[128,256,128]{1,2,0:T(8,128)} %convolution_bitcast_fusion.1), slice={[0:127], [0:256], [0:128]} | slice | bytes 33292288 | tf_op jit(solution)/shard_map/slice | solution.py:157
  200.8 6.0 %slice.53 = f32[127,256,128]{1,2,0:T(8,128)} slice(f32[128,256,128]{1,2,0:T(8,128)S(1)} %convolution_bitcast_fusion), slice={[1:128], [0:256], [0:128]} | slice | bytes 33292288 | tf_op jit(solution)/shard_map/slice | solution.py:158
  206.8 0.2 convolution_bitcast_fusion.4
  207.0 0.2 convolution_bitcast_fusion.3
  207.2 0.6 copy.66
  207.8 1.3 fusion.18
  209.1 11.5 %fusion.4 = f32[2,128,64,256]{3,1,2,0:T(8,128)} fusion(bf16[64,256,256]{2,1,0:T(8,128)(2,1)} %param.19, bf16[2,256,128,1]{2,0,1,3:T(2,128)(2,1)S(1)} %fusion.18), kind=kOutput, calls=%fused_computation.9 | convolution fusion | flops 2147483648 | bytes 25296896 | tf_op jit(solution)/shard_map/spq,bqt->bspt/dot_general | solution.py:141
  220.6 23.8 %fusion.3 = bf16[128,256,128]{1,2,0:T(8,128)(2,1)} fusion(f32[127,256,128]{1,2,0:T(8,128)} %slice.52, f32[1,256,128]{1,2,0:T(8,128)S(1)} %convolution_bitcast_fusion.4, f32[1,256,128]{1,2,0:T(8,128)S(1)} %convolution_bitcast_fusion.3, f32[127,256,128]{1,2,0:T(8,128)} %slice.53, f32[2,128,64,256]{3,1,2,0:T(8,128)} %fusion.4, ...), kind=kOutput, calls=%fused_computation.5 | convolution fusion | flops 2181038080 | bytes 67240960 | tf_op jit(solution)/shard_map/pr,lrt->lpt/dot_general | solution.py:146
  244.4 11.9 %copy.69 = bf16[128,256,128]{2,1,0:T(8,128)(2,1)} copy(bf16[128,256,128]{1,2,0:T(8,128)(2,1)} %fusion.3) | data formatting | bytes 16777216 | tf_op jit(solution)/shard_map/convert_element_type | solution.py:164
  (28 shorter events, 0.3 us)
Async XLA Ops:
  0.0 126.4 %copy-start = (f32[32,64,256]{2,1,0:T(8,128)S(1)}, f32[32,64,256]{2,1,0:T(8,128)}, u32[]{:S(2)}) copy-start(f32[32,64,256]{2,1,0:T(8,128)} %param.17) | copy-start | bytes 6291460
  0.0 8.5 %copy-start.7 = (s32[128]{0:T(128)S(1)}, s32[128]{0:T(128)}, u32[]{:S(2)}) copy-start(s32[128]{0:T(128)} %param.11) | copy-start | bytes 1540
  8.3 20.7 %copy-start.4 = (s32[128,2]{0,1:T(2,128)S(1)}, s32[128,2]{0,1:T(2,128)}, u32[]{:S(2)}) copy-start(s32[128,2]{0,1:T(2,128)} %param.12) | copy-start | bytes 3076
  8.3 20.7 %copy-start.2 = (f32[128]{0:T(128)S(1)}, f32[128]{0:T(128)}, u32[]{:S(2)}) copy-start(f32[128]{0:T(128)} %param.18) | copy-start | bytes 1540
  12.7 116.6 %all-to-all-start = ((f32[16,16,32,128]{3,2,1,0:T(8,128)}), f32[16,16,32,128]{3,2,1,0:T(8,128)}, u32[]{:S(2)}, u32[]{:S(2)}) async-start(f32[16,16,32,128]{3,2,1,0:T(8,128)} %bitcast.97), calls=%async_computation | async-start | bytes 8388608 | tf_op jit(solution)/shard_map/all_to_all | solution.py:19
  21.0 185.7 %collective-permute-start = (bf16[1,256,128]{2,1,0:T(8,128)(2,1)S(1)}, bf16[1,256,128]{2,1,0:T(8,128)(2,1)S(1)}, u32[]{:S(2)}, u32[]{:S(2)}) collective-permute-start(bf16[1,256,128]{2,1,0:T(8,128)(2,1)S(1)} %get-tuple-element.6), channel_id=1, source_target_pairs={{0,1},{1,2},{2,3},{3,4},{4,5},{5,6},{6,7},{7,8},{8,9},{9,10},{10,1... | collective-permute-start | bytes 196616 | tf_op jit(solution)/shard_map/ppermute | solution.py:72
  24.4 182.6 %collective-permute-start.1 = (bf16[1,256,128]{2,1,0:T(8,128)(2,1)S(1)}, bf16[1,256,128]{2,1,0:T(8,128)(2,1)S(1)}, u32[]{:S(2)}, u32[]{:S(2)}) collective-permute-start(bf16[1,256,128]{2,1,0:T(8,128)(2,1)S(1)} %get-tuple-element.5), channel_id=1, source_target_pairs={{1,0},{2,1},{3,2},{4,3},{5,4},{6,5},{7,6},{8,7},{9,8},{10,9},{11,1... | collective-permute-start | bytes 196616 | tf_op jit(solution)/shard_map/ppermute | solution.py:75
  29.1 97.2 %copy-start.5 = (s32[32]{0:T(128)S(1)}, s32[32]{0:T(128)}, u32[]{:S(2)}) copy-start(s32[32]{0:T(128)} %param.16) | copy-start | bytes 388
  29.1 97.3 %copy-start.6 = (s32[32,64]{1,0:T(8,128)S(1)}, s32[32,64]{1,0:T(8,128)}, u32[]{:S(2)}) copy-start(s32[32,64]{1,0:T(8,128)} %param.15) | copy-start | bytes 24580
  131.9 39.6 %copy-start.3 = (bf16[3,256,256]{2,1,0:T(8,128)(2,1)S(1)}, bf16[3,256,256]{2,1,0:T(8,128)(2,1)}, u32[]{:S(2)}) copy-start(bf16[3,256,256]{2,1,0:T(8,128)(2,1)} %param.13) | copy-start | bytes 1179652
  166.1 41.1 %all-to-all-start.1 = ((bf16[16,32,16,128]{3,2,1,0:T(8,128)(2,1)}), bf16[16,32,16,128]{3,2,1,0:T(8,128)(2,1)S(1)}, u32[]{:S(2)}, u32[]{:S(2)}) async-start(bf16[16,32,16,128]{3,2,1,0:T(8,128)(2,1)} %broadcast_in_dim.36), calls=%async_computation.1 | async-start | bytes 4194304 | tf_op jit(solution)/shard_map/all_to_all | solution.py:58
  220.6 35.7 %copy-start.1 = (f32[32,64,256]{2,1,0:T(8,128)S(1)}, f32[32,64,256]{2,1,0:T(8,128)}, u32[]{:S(2)}) copy-start(f32[32,64,256]{2,1,0:T(8,128)} %param.17) | copy-start | bytes 6291460
where the time goes:
time: 257 us; the launch traced here: 256 us
  local copies, waits for them, and re-layouts  131 us (51%)
  matrix products  70.7 us (28%)
  blocking collectives  30.8 us (12%)
  starting transfers between devices  20.9 us (8%)
  other arithmetic  2.84 us (1%)
    gather x1, local copies, waits for them, and re-layouts, time_matrix(): kernel[jnp.clip(sample_lag, 0, length - 1)]  97.2 us
    all_gather x4, blocking collectives, all_blocks(): tiles = lax.all_gather(tiles, axes[k], axis=0, tiled=True)  30.8 us
    dot_general x1, matrix products, per_device(): jnp.einsum('pr,lrt->lpt', near_blocks[0], currents, preferred_element_typ...  23.8 us
    convert_element_type x1, local copies, waits for them, and re-layouts, per_device(): return (near_field + far_field).astype(jnp.bfloat16)  11.9 us
    slice x1, local copies, waits for them, and re-layouts, per_device(): before_term = jnp.concatenate([before_rim[None], before_all[:-1]], axis=0)  11.8 us
    dot_general x1, matrix products, per_device(): jnp.einsum('spq,bqt->bspt', map_block, selected, preferred_element_type=j...  11.5 us
    dot_general x1, matrix products, per_device(): jnp.einsum('pr,lrt->lpt', near_blocks[1], currents, preferred_element_typ...  11.5 us
    dot_general x1, matrix products, per_device(): jnp.einsum('sqp,bspt->bqt', map_block, leaf_runs, preferred_element_type=...  8.31 us
  transfers between devices with their start and end apart: 4, of which 0 were waited for; matrix products, arithmetic and copies ran while one was open for 56% of the time, Pallas kernels for 0%

commit v1 on v0

--- a/solution.py
+++ b/solution.py
@@ -28,7 +28,9 @@
 def all_blocks(array, axes, sequence):
     tiles = array[None]
     for k in sequence:
-        tiles = lax.all_gather(tiles, axes[k], axis=0, tiled=True)
+        tiles = jnp.concatenate(
+            lax.all_to_all(jnp.stack([tiles] * lax.axis_size(axes[k])), axes[k], 0, 0), axis=0
+        )
     held = [lax.axis_size(axes[k]) for k in reversed(sequence)]
     tiles = tiles.reshape(*held, *array.shape)
     turned = sorted(range(len(sequence)), key=lambda place: sequence[len(sequence) - 1 - place])

time: 257 us -> 387 us (1.51)
  local copies, waits for them, and re-layouts: 131 us -> 203 us
  waiting for transfers between devices: 0.01 us -> 49.1 us
  starting transfers between devices: 20.9 us -> 45 us
  blocking collectives: 30.8 us -> 7.99 us
  matrix products: 70.7 us -> 75.7 us
    gather x1, local copies, waits for them, and re-layouts: 97.2 us -> 167 us  [time_matrix(): kernel[jnp.clip(sample_lag, 0, length - 1)]]
    all_to_all x1, waiting for transfers between devices: 0.01 us -> 45.1 us  [summed_on_arrival(): lax.all_to_all(tiles, axis, split_axis=0, concat_axis=0, tiled=True)]
    all_gather x4 -> x0, blocking collectives: 30.8 us -> none  [all_blocks(): tiles = lax.all_gather(tiles, axes[k], axis=0, tiled=True)]
    all_to_all x1, starting transfers between devices: 5.51 us -> 19.2 us  [sent_to_all(): lax.all_to_all(jnp.broadcast_to(array[None], (devices, *array.shape)), ax...]
    all_to_all x0 -> x2, starting transfers between devices: none -> 10.2 us  [all_blocks(): lax.all_to_all(jnp.stack([tiles] * lax.axis_size(axes[k])), axes[k], 0, 0)]
    all_to_all x0 -> x2, blocking collectives: none -> 7.99 us  [all_blocks(): lax.all_to_all(jnp.stack([tiles] * lax.axis_size(axes[k])), axes[k], 0, 0)]
    all_to_all x0 -> x2, waiting for transfers between devices: none -> 3.92 us  [all_blocks(): lax.all_to_all(jnp.stack([tiles] * lax.axis_size(axes[k])), axes[k], 0, 0)]
  transfers between devices with their start and end apart: 4 -> 6, of which waited for: 0 -> 2; matrix products, arithmetic and copies ran while one was open for 56% -> 57% of each run, Pallas kernels for 0% -> 0%
where the time goes in v1:
time: 387 us; the launch traced here: 384 us
  local copies, waits for them, and re-layouts  203 us (52%)
  matrix products  75.7 us (20%)
  waiting for transfers between devices  49.1 us (13%)
  starting transfers between devices  45 us (12%)
  blocking collectives  7.99 us (2%)
    gather x1, local copies, waits for them, and re-layouts, time_matrix(): kernel[jnp.clip(sample_lag, 0, length - 1)]  167 us
    all_to_all x1, waiting for transfers between devices, summed_on_arrival(): lax.all_to_all(tiles, axis, split_axis=0, concat_axis=0, tiled=True)  45.1 us
    dot_general x1, matrix products, per_device(): jnp.einsum('pr,lrt->lpt', near_blocks[0], currents, preferred_element_typ...  23.8 us
    all_to_all x1, starting transfers between devices, sent_to_all(): lax.all_to_all(jnp.broadcast_to(array[None], (devices, *array.shape)), ax...  19.2 us
    convert_element_type x1, local copies, waits for them, and re-layouts, per_device(): return (near_field + far_field).astype(jnp.bfloat16)  11.9 us
    slice x1, local copies, waits for them, and re-layouts, per_device(): before_term = jnp.concatenate([before_rim[None], before_all[:-1]], axis=0)  11.9 us
    dot_general x1, matrix products, per_device(): jnp.einsum('spq,bqt->bspt', map_block, selected, preferred_element_type=j...  11.5 us
    dot_general x1, matrix products, per_device(): jnp.einsum('pr,lrt->lpt', near_blocks[1], currents, preferred_element_typ...  11.5 us
  transfers between devices with their start and end apart: 6, of which 2 were waited for; matrix products, arithmetic and copies ran while one was open for 57% of the time, Pallas kernels for 0%

profile of v1, /device:TPU:34, one launch (start us, length us, event | category | flops | bytes accessed | tf_op | source)
XLA Modules:
  0.0 384.1 jit_solution(7514577259045921569)
XLA Ops:
  0.0 8.3 %fusion.12 = f32[2,256,128]{1,2,0:T(8,128)S(1)} fusion(bf16[2,64,256,128]{3,2,1,0:T(8,128)(2,1)} %bitcast.97, bf16[64,256,256]{2,1,0:T(8,128)(2,1)} %param.14), kind=kOutput, calls=%fused_computation.18 | convolution fusion | flops 2147483648 | bytes 17039360 | tf_op jit(solution)/shard_map/sqp,bspt->bqt/dot_general | solution.py:116
  8.7 3.9 %fusion.47 = f32[256,128,32]{1,2,0:T(8,128)} fusion(f32[2,256,128]{2,0,1:T(2,128)S(1)} %copy.47, s32[2]{0:T(128)S(1)} %slice_reduce_fusion), kind=kOutput, calls=%fused_computation.59 | convolution fusion | flops 25165888 | bytes 4456456 | tf_op jit(solution)/shard_map/bc,bqt->qct/dot_general | solution.py:118
  12.6 7.6 %all-to-all-start = ((f32[16,16,32,128]{3,2,1,0:T(8,128)}), f32[16,16,32,128]{3,2,1,0:T(8,128)}, u32[]{:S(2)}, u32[]{:S(2)}) async-start(f32[16,16,32,128]{3,2,1,0:T(8,128)} %bitcast.98), calls=%async_computation | async-start | bytes 8388608 | tf_op jit(solution)/shard_map/all_to_all | solution.py:19
  20.3 1.5 fusion.55
  21.8 3.4 collective-permute-start
  25.2 4.6 %collective-permute-start.1 = (bf16[1,256,128]{2,1,0:T(8,128)(2,1)}, bf16[1,256,128]{2,1,0:T(8,128)(2,1)}, u32[]{:S(2)}, u32[]{:S(2)}) collective-permute-start(bf16[1,256,128]{2,1,0:T(8,128)(2,1)} %get-tuple-element.5), channel_id=1, source_target_pairs={{1,0},{2,1},{3,2},{4,3},{5,4},{6,5},{7,6},{8,7},{9,8},{10,9},{11,1... | collective-permute-start | bytes 196616 | tf_op jit(solution)/shard_map/ppermute | solution.py:77
  29.8 45.1 %all-to-all-done = f32[16,16,32,128]{3,2,1,0:T(8,128)} async-done(((f32[16,16,32,128]{3,2,1,0:T(8,128)}), f32[16,16,32,128]{3,2,1,0:T(8,128)}, u32[]{:S(2)}, u32[]{:S(2)}) %all-to-all-start) | async-done | bytes 4194336 | tf_op jit(solution)/shard_map/all_to_all | solution.py:19
  74.9 2.6 reduce_sum.9
  77.6 3.8 all_to_all.30
  81.4 0.7 stack.14
  82.2 5.4 %all-to-all-start.3 = ((bf16[4,1,16,16,128]{4,3,2,1,0:T(8,128)(2,1)}), bf16[4,1,16,16,128]{4,3,2,1,0:T(8,128)(2,1)S(1)}, u32[]{:S(2)}, u32[]{:S(2)}) async-start(bf16[4,1,16,16,128]{4,3,2,1,0:T(8,128)(2,1)} %stack.14), calls=%async_computation.3 | async-start | bytes 524288 | tf_op jit(solution)/shard_map/all_to_all | solution.py:32
  87.7 167.4 %gather_fusion = f32[16384]{0:T(1024)} fusion(f32[128]{0:T(128)S(1)} %copy-done.2, s32[16384]{0:T(1024)S(1)} %fusion.39), kind=kCustom, calls=%fused_computation | custom fusion | bytes 196608 | tf_op jit(solution)/shard_map/gather | solution.py:86
  255.2 4.2 %all_to_all.31 = bf16[2,4,16,16,128]{4,3,1,2,0:T(8,128)(2,1)S(1)} all-to-all(bf16[2,4,16,16,128]{4,3,1,2,0:T(8,128)(2,1)S(1)} %copy.50), channel_id=1, replica_groups=mesh['box_0'=4,'box_1'=2,'dir'=16] {'box_1'}, dimensions={0} | all-to-all | bytes 1048576 | tf_op jit(solution)/shard_map/all_to_all | solution.py:32
  259.4 0.9 stack.13
  260.2 4.8 %all-to-all-start.2 = ((bf16[4,2,16,16,128]{4,3,1,2,0:T(8,128)(2,1)}), bf16[4,2,16,16,128]{4,3,1,2,0:T(8,128)(2,1)S(1)}, u32[]{:S(2)}, u32[]{:S(2)}) async-start(bf16[4,2,16,16,128]{4,3,1,2,0:T(8,128)(2,1)} %stack.13), calls=%async_computation.2 | async-start | bytes 1048576 | tf_op jit(solution)/shard_map/all_to_all | solution.py:32
  265.1 4.3 %fusion.10 = f32[32,256,16]{1,2,0:T(8,128)} fusion(f32[32,64,256]{2,1,0:T(8,128)S(1)} %copy-done, s32[]{:T(128)S(6)} %select_n.17, f32[32,64]{1,0:T(8,128)S(1)} %fusion.45, s32[32,64]{1,0:T(8,128)} %param.15), kind=kOutput, calls=%fused_computation.15 | convolution fusion | flops 101711872 | bytes 1597444 | tf_op jit(solution)/shard_map/cfs,cfq->csq/dot_general | solution.py:126
  269.4 3.9 %all-to-all-done.2 = bf16[4,2,16,16,128]{4,3,1,2,0:T(8,128)(2,1)S(1)} async-done(((bf16[4,2,16,16,128]{4,3,1,2,0:T(8,128)(2,1)}), bf16[4,2,16,16,128]{4,3,1,2,0:T(8,128)(2,1)S(1)}, u32[]{:S(2)}, u32[]{:S(2)}) %all-to-all-start.2) | async-done | bytes 524320 | tf_op jit(solution)/shard_map/all_to_all | solution.py:32
  273.5 1.8 convolution_bitcast_fusion.2
  275.4 1.3 convolution_convert_fusion
  276.7 1.7 broadcast_in_dim.13
  278.4 19.2 %all-to-all-start.5 = ((bf16[16,32,16,128]{3,2,1,0:T(8,128)(2,1)}), bf16[16,32,16,128]{3,2,1,0:T(8,128)(2,1)S(1)}, u32[]{:S(2)}, u32[]{:S(2)}) async-start(bf16[16,32,16,128]{3,2,1,0:T(8,128)(2,1)} %broadcast_in_dim.13), calls=%async_computation.5 | async-start | bytes 4194304 | tf_op jit(solution)/shard_map/all_to_all | solution.py:60
  297.6 11.5 %convolution_bitcast_fusion.1 = f32[128,256,128]{1,2,0:T(8,128)} fusion(bf16[128,256,128]{2,1,0:T(8,128)(2,1)} %param.10, bf16[3,256,256]{2,1,0:T(8,128)(2,1)S(1)} %copy-done.3), kind=kOutput, calls=%fused_computation.8 | convolution fusion | flops 2147483648 | bytes 25296896 | tf_op jit(solution)/shard_map/pr,lrt->lpt/dot_general | solution.py:151
  309.1 5.8 %convolution_bitcast_fusion = f32[128,256,128]{1,2,0:T(8,128)S(1)} fusion(bf16[128,256,128]{2,1,0:T(8,128)(2,1)} %param.10, bf16[3,256,256]{2,1,0:T(8,128)(2,1)S(1)} %copy-done.3), kind=kOutput, calls=%fused_computation.7 | convolution fusion | flops 2147483648 | bytes 25296896 | tf_op jit(solution)/shard_map/pr,lrt->lpt/dot_general | solution.py:154
  314.9 11.9 %slice.52 = f32[127,256,128]{1,2,0:T(8,128)} slice(f32[128,256,128]{1,2,0:T(8,128)} %convolution_bitcast_fusion.1), slice={[0:127], [0:256], [0:128]} | slice | bytes 33292288 | tf_op jit(solution)/shard_map/slice | solution.py:159
  326.8 6.0 %slice.53 = f32[127,256,128]{1,2,0:T(8,128)} slice(f32[128,256,128]{1,2,0:T(8,128)S(1)} %convolution_bitcast_fusion), slice={[1:128], [0:256], [0:128]} | slice | bytes 33292288 | tf_op jit(solution)/shard_map/slice | solution.py:160
  332.9 1.1 convolution_bitcast_fusion.4
  333.9 1.1 convolution_bitcast_fusion.3
  335.0 0.6 copy.55
  335.6 1.3 fusion.18
  336.9 11.5 %fusion.4 = f32[2,128,64,256]{3,1,2,0:T(8,128)} fusion(bf16[64,256,256]{2,1,0:T(8,128)(2,1)} %param.19, bf16[2,256,128,1]{2,0,1,3:T(2,128)(2,1)S(1)} %fusion.18), kind=kOutput, calls=%fused_computation.9 | convolution fusion | flops 2147483648 | bytes 25296896 | tf_op jit(solution)/shard_map/spq,bqt->bspt/dot_general | solution.py:143
  348.4 23.8 %fusion.3 = bf16[128,256,128]{1,2,0:T(8,128)(2,1)} fusion(f32[127,256,128]{1,2,0:T(8,128)} %slice.52, f32[1,256,128]{1,2,0:T(8,128)S(1)} %convolution_bitcast_fusion.4, f32[1,256,128]{1,2,0:T(8,128)S(1)} %convolution_bitcast_fusion.3, f32[127,256,128]{1,2,0:T(8,128)} %slice.53, f32[2,128,64,256]{3,1,2,0:T(8,128)} %fusion.4, ...), kind=kOutput, calls=%fused_computation.5 | convolution fusion | flops 2181038080 | bytes 67240960 | tf_op jit(solution)/shard_map/pr,lrt->lpt/dot_general | solution.py:148
  372.2 11.9 %copy.58 = bf16[128,256,128]{2,1,0:T(8,128)(2,1)} copy(bf16[128,256,128]{1,2,0:T(8,128)(2,1)} %fusion.3) | data formatting | bytes 16777216 | tf_op jit(solution)/shard_map/convert_element_type | solution.py:166
  (34 shorter events, 0.8 us)
Async XLA Ops:
  0.0 265.1 %copy-start = (f32[32,64,256]{2,1,0:T(8,128)S(1)}, f32[32,64,256]{2,1,0:T(8,128)}, u32[]{:S(2)}) copy-start(f32[32,64,256]{2,1,0:T(8,128)} %param.17) | copy-start | bytes 6291460
  0.0 8.5 %copy-start.6 = (s32[128]{0:T(128)S(1)}, s32[128]{0:T(128)}, u32[]{:S(2)}) copy-start(s32[128]{0:T(128)} %param.11) | copy-start | bytes 1540
  8.3 21.4 %copy-start.4 = (s32[128,2]{0,1:T(2,128)S(1)}, s32[128,2]{0,1:T(2,128)}, u32[]{:S(2)}) copy-start(s32[128,2]{0,1:T(2,128)} %param.12) | copy-start | bytes 3076
  12.6 75.0 %copy-start.2 = (f32[128]{0:T(128)S(1)}, f32[128]{0:T(128)}, u32[]{:S(2)}) copy-start(f32[128]{0:T(128)} %param.18) | copy-start | bytes 1540
  12.6 62.3 %all-to-all-start = ((f32[16,16,32,128]{3,2,1,0:T(8,128)}), f32[16,16,32,128]{3,2,1,0:T(8,128)}, u32[]{:S(2)}, u32[]{:S(2)}) async-start(f32[16,16,32,128]{3,2,1,0:T(8,128)} %bitcast.98), calls=%async_computation | async-start | bytes 8388608 | tf_op jit(solution)/shard_map/all_to_all | solution.py:19
  21.8 311.1 %collective-permute-start = (bf16[1,256,128]{2,1,0:T(8,128)(2,1)}, bf16[1,256,128]{2,1,0:T(8,128)(2,1)}, u32[]{:S(2)}, u32[]{:S(2)}) collective-permute-start(bf16[1,256,128]{2,1,0:T(8,128)(2,1)} %get-tuple-element.6), channel_id=1, source_target_pairs={{0,1},{1,2},{2,3},{3,4},{4,5},{5,6},{6,7},{7,8},{8,9},{9,10},{10,1... | collective-permute-start | bytes 196616 | tf_op jit(solution)/shard_map/ppermute | solution.py:74
  25.2 308.8 %collective-permute-start.1 = (bf16[1,256,128]{2,1,0:T(8,128)(2,1)}, bf16[1,256,128]{2,1,0:T(8,128)(2,1)}, u32[]{:S(2)}, u32[]{:S(2)}) collective-permute-start(bf16[1,256,128]{2,1,0:T(8,128)(2,1)} %get-tuple-element.5), channel_id=1, source_target_pairs={{1,0},{2,1},{3,2},{4,3},{5,4},{6,5},{7,6},{8,7},{9,8},{10,9},{11,1... | collective-permute-start | bytes 196616 | tf_op jit(solution)/shard_map/ppermute | solution.py:77
  82.2 172.9 %all-to-all-start.3 = ((bf16[4,1,16,16,128]{4,3,2,1,0:T(8,128)(2,1)}), bf16[4,1,16,16,128]{4,3,2,1,0:T(8,128)(2,1)S(1)}, u32[]{:S(2)}, u32[]{:S(2)}) async-start(bf16[4,1,16,16,128]{4,3,2,1,0:T(8,128)(2,1)} %stack.14), calls=%async_computation.3 | async-start | bytes 524288 | tf_op jit(solution)/shard_map/all_to_all | solution.py:32
  87.6 177.4 %copy-start.5 = (s32[32]{0:T(128)S(1)}, s32[32]{0:T(128)}, u32[]{:S(2)}) copy-start(s32[32]{0:T(128)} %param.16) | copy-start | bytes 388
  259.4 38.2 %copy-start.3 = (bf16[3,256,256]{2,1,0:T(8,128)(2,1)S(1)}, bf16[3,256,256]{2,1,0:T(8,128)(2,1)}, u32[]{:S(2)}) copy-start(bf16[3,256,256]{2,1,0:T(8,128)(2,1)} %param.13) | copy-start | bytes 1179652
  260.2 13.1 %all-to-all-start.2 = ((bf16[4,2,16,16,128]{4,3,1,2,0:T(8,128)(2,1)}), bf16[4,2,16,16,128]{4,3,1,2,0:T(8,128)(2,1)S(1)}, u32[]{:S(2)}, u32[]{:S(2)}) async-start(bf16[4,2,16,16,128]{4,3,1,2,0:T(8,128)(2,1)} %stack.13), calls=%async_computation.2 | async-start | bytes 1048576 | tf_op jit(solution)/shard_map/all_to_all | solution.py:32
  278.4 56.6 %all-to-all-start.5 = ((bf16[16,32,16,128]{3,2,1,0:T(8,128)(2,1)}), bf16[16,32,16,128]{3,2,1,0:T(8,128)(2,1)S(1)}, u32[]{:S(2)}, u32[]{:S(2)}) async-start(bf16[16,32,16,128]{3,2,1,0:T(8,128)(2,1)} %broadcast_in_dim.13), calls=%async_computation.5 | async-start | bytes 4194304 | tf_op jit(solution)/shard_map/all_to_all | solution.py:60
  348.4 35.7 %copy-start.1 = (f32[32,64,256]{2,1,0:T(8,128)S(1)}, f32[32,64,256]{2,1,0:T(8,128)}, u32[]{:S(2)}) copy-start(f32[32,64,256]{2,1,0:T(8,128)} %param.17) | copy-start | bytes 6291460
